TPU v7x, 128 devices: a whole 4x4x4 slice. The times are simulated.
128 devices in a mesh: wide: 16 (over x_hi, z, core), node: 8 (over x_lo, y).
Axes of the slice: x: 4 (x_hi: 2, x_lo: 2; x = x_hi * 2 + x_lo), y: 4, z: 4, core: 2. Of those that a mesh axis runs over, the one named last changes fastest.
Arguments:
- tokens: bfloat16 [12288, 3072], P('wide', 'node'), may hold values from -6 to 6
- target: bfloat16 [12288, 3072], P('wide', 'node'), may hold values from -6 to 6
- mod_table: bfloat16 [32, 3072], P(None, 'node'), may hold values from -1.5 to 1.5
- adv_table: float32 [32, 16], replicated, may hold values from 0.25 to 4
- w_up: bfloat16 [3072, 7168], P('wide', 'node'), may hold values from -0.109375 to 0.109375
- w_down_t: bfloat16 [3072, 7168], P('wide', 'node'), may hold values from -0.0625 to 0.0625
- bins: int32 [48], P('wide'), may hold values from 0 to 31
- groups: int32 [48], P('wide'), may hold values from 0 to 15
Outputs:
- grad_tokens: float32 [12288, 3072], P('wide', 'node')
- grad_up: float32 [3072, 7168], P('wide', 'node')
- grad_down: float32 [3072, 7168], P('wide', 'node')
All inputs are finite; a program needn't handle non-finite values.
Results may differ from a plain program's by a relative error of at most 0.02.
Values may be sent and summed in bfloat16 or wider, within the bound.
A program may use at most 128 MiB of HBM per device.

v0:
```python
import jax
import jax.numpy as jnp
from jax import lax
from jax.sharding import PartitionSpec as P


def gelu_tanh(value):
    return jax.nn.gelu(value, approximate=True)


def contract_last(left, right):
    return lax.dot_general(
        left, right, (((1,), (1,)), ((), ())), preferred_element_type=jnp.float32
    )


def on_device(tokens, target, mod_table, adv_table, w_up, w_down_t, bins, groups):
    full_tok, full_mod = (
        lax.all_gather(tokens, "node", axis=1, tiled=True),
        lax.all_gather(mod_table, "node", axis=1, tiled=True),
    )
    rows = tokens.shape[0]
    micro = bins.shape[0]
    seq = rows // micro
    width = full_tok.shape[1]
    local_width = tokens.shape[1]
    bin_hot = (bins[:, None] == jnp.arange(adv_table.shape[0])[None, :]).astype(jnp.float32)
    grp_hot = (groups[:, None] == jnp.arange(adv_table.shape[1])[None, :]).astype(jnp.float32)
    high = lax.Precision.HIGHEST
    gain_full = 1.0 + jnp.dot(bin_hot, full_mod.astype(jnp.float32), precision=high)
    gain_local = 1.0 + jnp.dot(bin_hot, mod_table.astype(jnp.float32), precision=high)
    weight = jnp.sum(jnp.dot(bin_hot, adv_table, precision=high) * grp_hot, axis=1)
    modulated = (
        (full_tok.reshape(micro, seq, width).astype(jnp.float32) * gain_full[:, None, :])
        .astype(jnp.bfloat16)
        .reshape(rows, width)
    )
    hidden_cols = w_up.shape[1]

    def fold_rows(left, piece):
        return jnp.dot(left, piece, preferred_element_type=jnp.float32)

    def map_rows(left, piece):
        return contract_last(left, piece)

    pre = fold_rows(modulated, lax.all_gather(w_up, "wide", axis=0, tiled=True))
    hidden = gelu_tanh(pre).astype(jnp.bfloat16)
    delta_part = map_rows(hidden, lax.all_gather(w_down_t, "wide", axis=0, tiled=True))
    delta = lax.psum_scatter(
        delta_part.astype(jnp.bfloat16), "node", scatter_dimension=1, tiled=True
    ).astype(jnp.float32)
    err = tokens.astype(jnp.float32) + delta - target.astype(jnp.float32)
    dpred = (err.reshape(micro, seq, local_width) * weight[:, None, None]).reshape(
        rows, local_width
    )
    dy = dpred.astype(jnp.bfloat16)
    dy_full = lax.all_gather(dy, "node", axis=1, tiled=True)
    pull = jax.vjp(gelu_tanh, pre)[1]
    dh = fold_rows(dy_full, lax.all_gather(w_down_t, "wide", axis=0, tiled=True))
    dpre = pull(dh)[0].astype(jnp.bfloat16)
    dmod_part = map_rows(dpre, lax.all_gather(w_up, "wide", axis=0, tiled=True))
    dmod = lax.psum_scatter(
        dmod_part.astype(jnp.bfloat16), "node", scatter_dimension=1, tiled=True
    ).astype(jnp.float32)
    grad_tokens = dpred + (gain_local[:, None, :] * dmod.reshape(micro, seq, local_width)).reshape(
        rows, local_width
    )
    scale = float(lax.axis_size("wide") * rows) ** (-0.5)
    term_up = lax.dot_general(
        modulated, dpre, (((0,), (0,)), ((), ())), preferred_element_type=jnp.float32
    )
    term_down = lax.dot_general(
        dy_full, hidden, (((0,), (0,)), ((), ())), preferred_element_type=jnp.float32
    )
    summed = lax.psum_scatter(
        (jnp.concatenate([term_up, term_down], axis=1) * scale).astype(jnp.bfloat16),
        "wide",
        scatter_dimension=0,
        tiled=True,
    ).astype(jnp.float32)
    grad_up = summed[:, :hidden_cols]
    grad_down = summed[:, hidden_cols:]
    return (grad_tokens, grad_up, grad_down)


def solution(mesh):
    return jax.shard_map(
        on_device,
        mesh=mesh,
        in_specs=(
            P("wide", "node"),
            P("wide", "node"),
            P(None, "node"),
            P(),
            P("wide", "node"),
            P("wide", "node"),
            P("wide"),
            P("wide"),
        ),
        out_specs=(P("wide", "node"), P("wide", "node"), P("wide", "node")),
        check_vma=False,
    )
```

profile of v0, /device:TPU:1, one launch (start us, length us, event | category | flops | bytes accessed | tf_op | source)
XLA Modules:
  0.0 538.0 jit_solution(9273582299312235300)
XLA Ops:
  9.4 25.2 %all_gather.18 = bf16[32,3072]{1,0:T(8,128)(2,1)S(1)} all-gather(bf16[32,384]{1,0:T(8,128)(2,1)} %param.10), channel_id=1, replica_groups=mesh['wide'=16,'node'=8] {'node'}, dimensions={1}, use_global_device_ids=true | all-gather | bytes 221184 | tf_op jit(solution)/shard_map/all_gather | solution.py:20
  35.5 36.5 %all-gather.5.cloned.1.call-done = bf16[768,3072]{1,0:T(8,128)(2,1)} async-done(((bf16[768,384]{1,0:T(8,128)(2,1)}), bf16[768,3072]{1,0:T(8,128)(2,1)}) %all-gather.5.cloned.1.call-update) | async-done | bytes 4718608 | tf_op jit(solution)/shard_map/all_gather | solution.py:19
  72.0 5.7 %fusion.1 = bf16[768,3072]{1,0:T(8,128)(2,1)} fusion(bf16[768,3072]{1,0:T(8,128)(2,1)} %all-gather.5.cloned.1.call-done, f32[3,3072]{1,0:T(4,128)S(1)} %convolution_add_fusion), kind=kLoop, calls=%fused_computation.3 | loop fusion | flops 7077888 | bytes 9474048 | tf_op jit(solution)/shard_map/convert_element_type | solution.py:35
  77.7 56.7 %all-gather.7.cloned.1.call-done = bf16[3072,896]{1,0:T(8,128)(2,1)} async-done(((bf16[192,896]{1,0:T(8,128)(2,1)}), bf16[3072,896]{1,0:T(8,128)(2,1)}) %all-gather.7.cloned.1.call-update) | async-done | bytes 5505040 | tf_op jit(solution)/shard_map/all_gather | solution.py:46
  134.3 8.5 %fusion.17 = f32[768,896]{1,0:T(8,128)S(1)} fusion(bf16[768,3072]{1,0:T(8,128)(2,1)} %fusion.1, bf16[3072,896]{1,0:T(8,128)(2,1)} %all-gather.7.cloned.1.call-done), kind=kOutput, calls=%fused_computation.31 | convolution fusion | flops 4227858432 | bytes 12976128 | tf_op jit(solution)/shard_map/dot_general | solution.py:41
  142.9 52.7 %all-gather.9.cloned.1.call-done = bf16[3072,896]{1,0:T(8,128)(2,1)} async-done(((bf16[192,896]{1,0:T(8,128)(2,1)}), bf16[3072,896]{1,0:T(8,128)(2,1)}) %all-gather.9.cloned.1.call-update) | async-done | bytes 5505040 | tf_op jit(solution)/shard_map/all_gather | solution.py:48
  195.6 9.4 %convolution_convert_fusion.1 = bf16[768,3072]{1,0:T(8,128)(2,1)} fusion(bf16[3072,896]{1,0:T(8,128)(2,1)} %all-gather.9.cloned.1.call-done, f32[768,896]{1,0:T(8,128)S(1)} %fusion.17), kind=kOutput, calls=%fused_computation.5 | convolution fusion | flops 4236410880 | bytes 12976128 | tf_op jit(solution)/shard_map/dot_general | solution.py:12
  205.0 6.6 %copy.15 = bf16[768,3072]{0,1:T(8,128)(2,1)} copy(bf16[768,3072]{1,0:T(8,128)(2,1)} %convolution_convert_fusion.1) | data formatting | bytes 9437184
  212.7 54.6 %reduce-scatter.10.cloned.1.call-done = bf16[384,768]{1,0:T(8,128)(2,1)} async-done(((bf16[3072,768]{1,0:T(8,128)(2,1)}), bf16[384,768]{1,0:T(8,128)(2,1)}) %reduce-scatter.10.cloned.1.call-update) | async-done | bytes 589840
  267.2 1.4 copy.16
  269.8 56.4 %all-gather.11.cloned.1.call-done = bf16[768,3072]{1,0:T(8,128)(2,1)} async-done(((bf16[768,384]{1,0:T(8,128)(2,1)}), bf16[768,3072]{1,0:T(8,128)(2,1)}) %all-gather.11.cloned.1.call-update) | async-done | bytes 4718608 | tf_op jit(solution)/shard_map/all_gather | solution.py:57
  326.1 10.0 %fusion.8 = bf16[768,896]{1,0:T(8,128)(2,1)S(1)} fusion(f32[768,896]{1,0:T(8,128)} %copy-done.7, bf16[768,3072]{1,0:T(8,128)(2,1)} %all-gather.11.cloned.1.call-done, bf16[3072,896]{1,0:T(8,128)(2,1)} %all-gather.9.cloned.1.call-done), kind=kOutput, calls=%fused_computation.15 | convolution fusion | flops 4241620992 | bytes 14352384 | tf_op jit(solution)/shard_map/dot_general | solution.py:41
  337.2 9.3 %convolution_convert_fusion = bf16[768,3072]{1,0:T(8,128)(2,1)} fusion(bf16[768,896]{1,0:T(8,128)(2,1)S(1)} %fusion.8, bf16[3072,896]{1,0:T(8,128)(2,1)} %all-gather.7.cloned.1.call-done), kind=kOutput, calls=%fused_computation.4 | convolution fusion | flops 4230217728 | bytes 11599872 | tf_op jit(solution)/shard_map/dot_general | solution.py:12
  346.5 6.6 %copy.17 = bf16[768,3072]{0,1:T(8,128)(2,1)} copy(bf16[768,3072]{1,0:T(8,128)(2,1)} %convolution_convert_fusion) | data formatting | bytes 9437184
  353.4 6.9 %fusion.18 = f32[3072,896]{0,1:T(8,128)S(1)} fusion(bf16[768,3072]{1,0:T(8,128)(2,1)} %fusion.1, bf16[768,896]{1,0:T(8,128)(2,1)} %copy-done.9), kind=kOutput, calls=%fused_computation.32 | convolution fusion | flops 4227858432 | bytes 17104896 | tf_op jit(solution)/shard_map/dot_general | solution.py:69
  360.3 7.1 %fusion.15 = f32[3072,896]{0,1:T(8,128)S(1)} fusion(bf16[768,3072]{1,0:T(8,128)(2,1)} %all-gather.11.cloned.1.call-done, f32[768,896]{1,0:T(8,128)S(1)} %copy-done.8), kind=kOutput, calls=%fused_computation.29 | convolution fusion | flops 4234051584 | bytes 18481152 | tf_op jit(solution)/shard_map/dot_general | solution.py:72
  367.4 6.3 %fusion = bf16[3072,1792]{0,1:T(8,128)(2,1)} fusion(f32[3072,896]{0,1:T(8,128)S(1)} %fusion.15, f32[3072,896]{0,1:T(8,128)S(1)} %fusion.18), kind=kLoop, calls=%fused_computation.1 | loop fusion | flops 16515072 | bytes 33030144 | tf_op jit(solution)/shard_map/convert_element_type | solution.py:76
  373.8 14.3 %copy.19 = bf16[3072,1792]{1,0:T(8,128)(2,1)} copy(bf16[3072,1792]{0,1:T(8,128)(2,1)} %fusion) | data formatting | bytes 22020096
  389.0 21.1 %reduce-scatter.12.cloned.1.call-done = bf16[384,768]{1,0:T(8,128)(2,1)} async-done(((bf16[3072,768]{1,0:T(8,128)(2,1)}), bf16[384,768]{1,0:T(8,128)(2,1)}) %reduce-scatter.12.cloned.1.call-update) | async-done | bytes 589840
  410.1 1.4 copy.18
  411.5 1.4 fusion.9
  412.9 114.4 %reduce-scatter.14.cloned.1.call-done = bf16[192,1792]{1,0:T(8,128)(2,1)} async-done(((bf16[3072,1792]{1,0:T(8,128)(2,1)}), bf16[192,1792]{1,0:T(8,128)(2,1)}) %reduce-scatter.14.cloned.1.call-update) | async-done | bytes 688144
  527.3 1.4 copy.20
  528.9 1.1 copy.14
  (42 shorter events, 8.7 us)
Async XLA Ops:
  7.2 204.5 %copy-start = (f32[32,16]{0,1:T(8,128)S(1)}, f32[32,16]{0,1:T(8,128)}, u32[]{:S(2)}) copy-start(f32[32,16]{0,1:T(8,128)} %param.11) | copy-start | bytes 6148
  7.2 64.8 %all-gather.5.cloned.1.call-start = ((), (), s32[]{:S(2)}) async-start(), calls=%async_computation.3 | async-start | bytes 5308416 | tf_op jit(solution)/shard_map/all_gather | solution.py:19
  7.9 126.4 %all-gather.7.cloned.1.call-start = ((), (), s32[]{:S(2)}) async-start(), calls=%async_computation.4 | async-start | bytes 5849088 | tf_op jit(solution)/shard_map/all_gather | solution.py:46
  8.7 186.9 %all-gather.9.cloned.1.call-start = ((), (), s32[]{:S(2)}) async-start(), calls=%async_computation.5 | async-start | bytes 5849088 | tf_op jit(solution)/shard_map/all_gather | solution.py:48
  9.4 257.8 %reduce-scatter.10.cloned.1.call-start = ((), (), s32[]{:S(2)}) async-start(), calls=%async_computation.7 | async-start | bytes 5308416
  142.8 62.1 %copy-start.7 = (f32[768,896]{1,0:T(8,128)}, f32[768,896]{1,0:T(8,128)S(1)}, u32[]{:S(2)}) copy-start(f32[768,896]{1,0:T(8,128)S(1)} %fusion.17) | copy-start | bytes 8257540
  211.6 0.7 copy-start.5
  211.6 0.7 copy-start.6
  211.6 57.0 %copy-start.2 = (bf16[768,384]{1,0:T(8,128)(2,1)S(1)}, bf16[768,384]{1,0:T(8,128)(2,1)}, u32[]{:S(2)}) copy-start(bf16[768,384]{1,0:T(8,128)(2,1)} %param.8) | copy-start | bytes 1769476
  211.6 57.0 %copy-start.3 = (bf16[768,384]{1,0:T(8,128)(2,1)S(1)}, bf16[768,384]{1,0:T(8,128)(2,1)}, u32[]{:S(2)}) copy-start(bf16[768,384]{1,0:T(8,128)(2,1)} %param.9) | copy-start | bytes 1769476
  211.6 114.5 %all-gather.11.cloned.1.call-start = ((), (), s32[]{:S(2)}) async-start(), calls=%async_computation.6 | async-start | bytes 5308416 | tf_op jit(solution)/shard_map/all_gather | solution.py:57
  269.7 140.4 %reduce-scatter.12.cloned.1.call-start = ((), (), s32[]{:S(2)}) async-start(), calls=%async_computation.8 | async-start | bytes 5308416
  336.1 1.1 copy-start.9
  353.1 174.1 %reduce-scatter.14.cloned.1.call-start = ((), (), s32[]{:S(2)}) async-start(), calls=%async_computation.9 | async-start | bytes 11698176
  353.4 7.0 %copy-start.8 = (f32[768,896]{1,0:T(8,128)S(1)}, f32[768,896]{1,0:T(8,128)}, u32[]{:S(2)}) copy-start(f32[768,896]{1,0:T(8,128)} %copy-done.7) | copy-start | bytes 8257540
  388.1 0.7 copy-start.4
  527.3 3.9 copy-start.1
Sparse Core Ops, SparseCore 0:
  9.7 62.2 all-gather.4
  74.4 59.8 all-gather.6
  136.8 58.7 all-gather.8
  211.8 55.4 reduce-scatter.9
  269.8 56.2 all-gather.10
  353.3 56.8 reduce-scatter.11
  414.5 112.7 reduce-scatter.13
where the time goes:
time: 539 us; the launch traced here: 538 us
  waiting for transfers between devices  394 us (73%)
  matrix products  52.5 us (10%)
  local copies, waits for them, and re-layouts  36.6 us (7%)
  blocking collectives  25.2 us (5%)
  other arithmetic  14.5 us (3%)
  between operations  14.3 us (3%)
    unnamed x10, waiting for transfers between devices  192 us
    all_gather x1, waiting for transfers between devices, on_device(): pre = fold_rows(modulated, lax.all_gather(w_up, 'wide', axis=0, tiled=True))  56.7 us
    all_gather x1, waiting for transfers between devices, on_device(): dy_full = lax.all_gather(dy, 'node', axis=1, tiled=True)  56.4 us
    all_gather x1, waiting for transfers between devices, on_device(): lax.all_gather(w_down_t, 'wide', axis=0, tiled=True)  52.7 us
    all_gather x1, waiting for transfers between devices, on_device(): lax.all_gather(tokens, 'node', axis=1, tiled=True)  36.5 us
    unnamed x28, local copies, waits for them, and re-layouts  36.4 us
    all_gather x1, blocking collectives, on_device(): lax.all_gather(mod_table, 'node', axis=1, tiled=True)  25.2 us
    dot_general x2, matrix products, contract_last(): lax.dot_general(left, right, (((1,), (1,)), ((), ())), preferred_element_...  18.7 us
  transfers between devices with their start and end apart: 7, of which 7 were waited for; matrix products, arithmetic and copies ran while one was open for 10% of the time, Pallas kernels for 0%

commit v1 on v0

--- a/solution.py
+++ b/solution.py
@@ -2,6 +2,13 @@
 import jax.numpy as jnp
 from jax import lax
 from jax.sharding import PartitionSpec as P
+
+
+def swapped_in(array, axis, dim):
+    n_dev = lax.axis_size(axis)
+    shards = jnp.stack([array for _ in range(n_dev)])
+    shards = lax.all_to_all(shards, axis, split_axis=0, concat_axis=0)
+    return jnp.concatenate(shards, axis=dim)
 
 
 def gelu_tanh(value):
@@ -45,7 +52,7 @@
 
     pre = fold_rows(modulated, lax.all_gather(w_up, "wide", axis=0, tiled=True))
     hidden = gelu_tanh(pre).astype(jnp.bfloat16)
-    delta_part = map_rows(hidden, lax.all_gather(w_down_t, "wide", axis=0, tiled=True))
+    delta_part = map_rows(hidden, swapped_in(w_down_t, "wide", 0))
     delta = lax.psum_scatter(
         delta_part.astype(jnp.bfloat16), "node", scatter_dimension=1, tiled=True
     ).astype(jnp.float32)

time: 539 us -> 598 us (1.11)
  blocking collectives: 25.2 us -> 132 us
  waiting for transfers between devices: 394 us -> 333 us
  starting transfers between devices: 0.46 us -> 9.88 us
    all_gather x1, blocking collectives: 25.2 us -> 132 us  [on_device(): lax.all_gather(mod_table, 'node', axis=1, tiled=True)]
    all_gather x1, waiting for transfers between devices: 36.5 us -> 0.02 us  [on_device(): lax.all_gather(tokens, 'node', axis=1, tiled=True)]
    all_gather x1, waiting for transfers between devices: 56.7 us -> 23 us  [on_device(): pre = fold_rows(modulated, lax.all_gather(w_up, 'wide', axis=0, tiled=True))]
    all_to_all x0 -> x1, starting transfers between devices: none -> 9.42 us  [swapped_in(): shards = lax.all_to_all(shards, axis, split_axis=0, concat_axis=0)]
    all_gather x1, waiting for transfers between devices: 52.7 us -> 60 us  [on_device(): lax.all_gather(w_down_t, 'wide', axis=0, tiled=True)]
    unnamed x28 -> x26, local copies, waits for them, and re-layouts: 36.4 us -> 34.9 us
  transfers between devices with their start and end apart: 7 -> 8, of which waited for: 7 -> 6; matrix products, arithmetic and copies ran while one was open for 10% -> 10% of each run, Pallas kernels for 0% -> 0%
where the time goes in v1:
time: 598 us; the launch traced here: 597 us
  waiting for transfers between devices  333 us (56%)
  blocking collectives  132 us (22%)
  matrix products  53.2 us (9%)
  local copies, waits for them, and re-layouts  39.2 us (7%)
  other arithmetic  15.1 us (3%)
  between operations  14.3 us (2%)
  starting transfers between devices  9.88 us (2%)
    unnamed x10, waiting for transfers between devices  193 us
    all_gather x1, blocking collectives, on_device(): lax.all_gather(mod_table, 'node', axis=1, tiled=True)  132 us
    all_gather x1, waiting for transfers between devices, on_device(): lax.all_gather(w_down_t, 'wide', axis=0, tiled=True)  60 us
    all_gather x1, waiting for transfers between devices, on_device(): dy_full = lax.all_gather(dy, 'node', axis=1, tiled=True)  56.9 us
    unnamed x26, local copies, waits for them, and re-layouts  34.9 us
    all_gather x1, waiting for transfers between devices, on_device(): pre = fold_rows(modulated, lax.all_gather(w_up, 'wide', axis=0, tiled=True))  23 us
    dot_general x2, matrix products, fold_rows(): return jnp.dot(left, piece, preferred_element_type=jnp.float32)  19.6 us
    dot_general x2, matrix products, contract_last(): lax.dot_general(left, right, (((1,), (1,)), ((), ())), preferred_element_...  18.9 us
  transfers between devices with their start and end apart: 8, of which 6 were waited for; matrix products, arithmetic and copies ran while one was open for 10% of the time, Pallas kernels for 0%

profile of v1, /device:TPU:1, one launch (start us, length us, event | category | flops | bytes accessed | tf_op | source)
XLA Modules:
  0.0 597.1 jit_solution(16226407181715458351)
XLA Ops:
  8.7 4.1 stack.2
  12.8 9.4 %all-to-all-start = ((bf16[16,192,896]{2,1,0:T(8,128)(2,1)}), bf16[16,192,896]{2,1,0:T(8,128)(2,1)}, u32[]{:S(2)}, u32[]{:S(2)}) async-start(bf16[16,192,896]{2,1,0:T(8,128)(2,1)} %stack.2), calls=%async_computation | async-start | bytes 11010048 | tf_op jit(solution)/shard_map/all_to_all | solution.py:10
  22.2 132.4 %all_gather.17 = bf16[32,3072]{1,0:T(8,128)(2,1)S(1)} all-gather(bf16[32,384]{1,0:T(8,128)(2,1)S(1)} %copy-done.4), channel_id=1, replica_groups=mesh['wide'=16,'node'=8] {'node'}, dimensions={1}, use_global_device_ids=true | all-gather | bytes 221184 | tf_op jit(solution)/shard_map/all_gather | solution.py:27
  154.8 6.4 %fusion.1 = bf16[768,3072]{1,0:T(8,128)(2,1)} fusion(bf16[768,3072]{1,0:T(8,128)(2,1)} %all-gather.5.cloned.1.call-done, f32[3,3072]{1,0:T(4,128)S(1)} %convolution_add_fusion), kind=kLoop, calls=%fused_computation.3 | loop fusion | flops 7077888 | bytes 9474048 | tf_op jit(solution)/shard_map/convert_element_type | solution.py:42
  161.2 23.0 %all-gather.7.cloned.1.call-done = bf16[3072,896]{1,0:T(8,128)(2,1)} async-done(((bf16[192,896]{1,0:T(8,128)(2,1)}), bf16[3072,896]{1,0:T(8,128)(2,1)}) %all-gather.7.cloned.1.call-update) | async-done | bytes 5505040 | tf_op jit(solution)/shard_map/all_gather | solution.py:53
  184.2 9.6 %fusion.17 = f32[768,896]{1,0:T(8,128)} fusion(bf16[768,3072]{1,0:T(8,128)(2,1)} %fusion.1, bf16[3072,896]{1,0:T(8,128)(2,1)} %all-gather.7.cloned.1.call-done), kind=kOutput, calls=%fused_computation.31 | convolution fusion | flops 4227858432 | bytes 12976128 | tf_op jit(solution)/shard_map/dot_general | solution.py:48
  193.8 9.6 %convolution_convert_fusion.1 = bf16[768,3072]{1,0:T(8,128)(2,1)} fusion(bf16[3072,896]{1,0:T(8,128)(2,1)} %bitcast.1, f32[768,896]{1,0:T(8,128)} %fusion.17), kind=kOutput, calls=%fused_computation.5 | convolution fusion | flops 4236410880 | bytes 12976128 | tf_op jit(solution)/shard_map/dot_general | solution.py:19
  203.5 6.7 %copy.15 = bf16[768,3072]{0,1:T(8,128)(2,1)} copy(bf16[768,3072]{1,0:T(8,128)(2,1)} %convolution_convert_fusion.1) | data formatting | bytes 9437184
  211.2 54.5 %reduce-scatter.10.cloned.1.call-done = bf16[384,768]{1,0:T(8,128)(2,1)} async-done(((bf16[3072,768]{1,0:T(8,128)(2,1)}), bf16[384,768]{1,0:T(8,128)(2,1)}) %reduce-scatter.10.cloned.1.call-update) | async-done | bytes 589840
  265.7 1.4 copy.16
  268.3 60.0 %all-gather.11.cloned.1.call-done = bf16[3072,896]{1,0:T(8,128)(2,1)} async-done(((bf16[192,896]{1,0:T(8,128)(2,1)}), bf16[3072,896]{1,0:T(8,128)(2,1)}) %all-gather.11.cloned.1.call-update) | async-done | bytes 5505040 | tf_op jit(solution)/shard_map/all_gather | solution.py:66
  328.3 56.9 %all-gather.9.cloned.1.call-done = bf16[768,3072]{1,0:T(8,128)(2,1)} async-done(((bf16[768,384]{1,0:T(8,128)(2,1)}), bf16[768,3072]{1,0:T(8,128)(2,1)}) %all-gather.9.cloned.1.call-update) | async-done | bytes 4718608 | tf_op jit(solution)/shard_map/all_gather | solution.py:64
  385.2 10.0 %fusion.8 = bf16[768,896]{1,0:T(8,128)(2,1)S(1)} fusion(f32[768,896]{1,0:T(8,128)} %fusion.17, bf16[768,3072]{1,0:T(8,128)(2,1)} %all-gather.9.cloned.1.call-done, bf16[3072,896]{1,0:T(8,128)(2,1)} %all-gather.11.cloned.1.call-done), kind=kOutput, calls=%fused_computation.15 | convolution fusion | flops 4241620992 | bytes 14352384 | tf_op jit(solution)/shard_map/dot_general | solution.py:48
  396.3 9.3 %convolution_convert_fusion = bf16[768,3072]{1,0:T(8,128)(2,1)} fusion(bf16[768,896]{1,0:T(8,128)(2,1)S(1)} %fusion.8, bf16[3072,896]{1,0:T(8,128)(2,1)} %all-gather.7.cloned.1.call-done), kind=kOutput, calls=%fused_computation.4 | convolution fusion | flops 4230217728 | bytes 11599872 | tf_op jit(solution)/shard_map/dot_general | solution.py:19
  405.6 6.6 %copy.17 = bf16[768,3072]{0,1:T(8,128)(2,1)} copy(bf16[768,3072]{1,0:T(8,128)(2,1)} %convolution_convert_fusion) | data formatting | bytes 9437184
  412.5 6.9 %fusion.18 = f32[3072,896]{0,1:T(8,128)S(1)} fusion(bf16[768,3072]{1,0:T(8,128)(2,1)} %fusion.1, bf16[768,896]{1,0:T(8,128)(2,1)} %copy-done.8), kind=kOutput, calls=%fused_computation.32 | convolution fusion | flops 4227858432 | bytes 17104896 | tf_op jit(solution)/shard_map/dot_general | solution.py:76
  419.4 7.1 %fusion.15 = f32[3072,896]{0,1:T(8,128)S(1)} fusion(bf16[768,3072]{1,0:T(8,128)(2,1)} %all-gather.9.cloned.1.call-done, f32[768,896]{1,0:T(8,128)S(1)} %copy-done.7), kind=kOutput, calls=%fused_computation.29 | convolution fusion | flops 4234051584 | bytes 18481152 | tf_op jit(solution)/shard_map/dot_general | solution.py:79
  426.5 6.3 %fusion = bf16[3072,1792]{0,1:T(8,128)(2,1)} fusion(f32[3072,896]{0,1:T(8,128)S(1)} %fusion.15, f32[3072,896]{0,1:T(8,128)S(1)} %fusion.18), kind=kLoop, calls=%fused_computation.1 | loop fusion | flops 16515072 | bytes 33030144 | tf_op jit(solution)/shard_map/convert_element_type | solution.py:83
  432.9 14.0 %copy.19 = bf16[3072,1792]{1,0:T(8,128)(2,1)} copy(bf16[3072,1792]{0,1:T(8,128)(2,1)} %fusion) | data formatting | bytes 22020096
  447.1 22.1 %reduce-scatter.12.cloned.1.call-done = bf16[384,768]{1,0:T(8,128)(2,1)} async-done(((bf16[3072,768]{1,0:T(8,128)(2,1)}), bf16[384,768]{1,0:T(8,128)(2,1)}) %reduce-scatter.12.cloned.1.call-update) | async-done | bytes 589840
  469.2 1.4 copy.18
  470.6 1.4 fusion.9
  472.0 114.4 %reduce-scatter.14.cloned.1.call-done = bf16[192,1792]{1,0:T(8,128)(2,1)} async-done(((bf16[3072,1792]{1,0:T(8,128)(2,1)}), bf16[192,1792]{1,0:T(8,128)(2,1)}) %reduce-scatter.14.cloned.1.call-update) | async-done | bytes 688144
  586.4 1.4 copy.20
  (43 shorter events, 7.8 us)
Async XLA Ops:
  7.2 203.6 %copy-start = (f32[32,16]{0,1:T(8,128)S(1)}, f32[32,16]{0,1:T(8,128)}, u32[]{:S(2)}) copy-start(f32[32,16]{0,1:T(8,128)} %param.11) | copy-start | bytes 6148
  7.2 147.7 %all-gather.5.cloned.1.call-start = ((), (), s32[]{:S(2)}) async-start(), calls=%async_computation.4 | async-start | bytes 5308416 | tf_op jit(solution)/shard_map/all_gather | solution.py:26
  7.9 176.3 %all-gather.7.cloned.1.call-start = ((), (), s32[]{:S(2)}) async-start(), calls=%async_computation.5 | async-start | bytes 5849088 | tf_op jit(solution)/shard_map/all_gather | solution.py:53
  12.8 9.5 %copy-start.4 = (bf16[32,384]{1,0:T(8,128)(2,1)S(1)}, bf16[32,384]{1,0:T(8,128)(2,1)}, u32[]{:S(2)}) copy-start(bf16[32,384]{1,0:T(8,128)(2,1)} %param.10) | copy-start | bytes 73732
  12.8 141.9 %copy-start.5 = (s32[3]{0:T(128)S(1)}, s32[3]{0:T(128)}, u32[]{:S(2)}) copy-start(s32[3]{0:T(128)} %param.14) | copy-start | bytes 40
  12.8 181.1 %all-to-all-start = ((bf16[16,192,896]{2,1,0:T(8,128)(2,1)}), bf16[16,192,896]{2,1,0:T(8,128)(2,1)}, u32[]{:S(2)}, u32[]{:S(2)}) async-start(bf16[16,192,896]{2,1,0:T(8,128)(2,1)} %stack.2), calls=%async_computation | async-start | bytes 11010048 | tf_op jit(solution)/shard_map/all_to_all | solution.py:10
  22.2 243.6 %reduce-scatter.10.cloned.1.call-start = ((), (), s32[]{:S(2)}) async-start(), calls=%async_computation.8 | async-start | bytes 5308416
  210.1 0.7 copy-start.6
  210.1 57.0 %copy-start.2 = (bf16[768,384]{1,0:T(8,128)(2,1)S(1)}, bf16[768,384]{1,0:T(8,128)(2,1)}, u32[]{:S(2)}) copy-start(bf16[768,384]{1,0:T(8,128)(2,1)} %param.8) | copy-start | bytes 1769476
  210.1 57.0 %copy-start.3 = (bf16[768,384]{1,0:T(8,128)(2,1)S(1)}, bf16[768,384]{1,0:T(8,128)(2,1)}, u32[]{:S(2)}) copy-start(bf16[768,384]{1,0:T(8,128)(2,1)} %param.9) | copy-start | bytes 1769476
  210.2 118.1 %all-gather.11.cloned.1.call-start = ((), (), s32[]{:S(2)}) async-start(), calls=%async_computation.7 | async-start | bytes 5849088 | tf_op jit(solution)/shard_map/all_gather | solution.py:66
  210.7 174.5 %all-gather.9.cloned.1.call-start = ((), (), s32[]{:S(2)}) async-start(), calls=%async_computation.6 | async-start | bytes 5308416 | tf_op jit(solution)/shard_map/all_gather | solution.py:64
  268.2 201.0 %reduce-scatter.12.cloned.1.call-start = ((), (), s32[]{:S(2)}) async-start(), calls=%async_computation.9 | async-start | bytes 5308416
  395.2 1.1 copy-start.8
  412.2 174.2 %reduce-scatter.14.cloned.1.call-start = ((), (), s32[]{:S(2)}) async-start(), calls=%async_computation.10 | async-start | bytes 11698176
  412.5 7.0 %copy-start.7 = (f32[768,896]{1,0:T(8,128)S(1)}, f32[768,896]{1,0:T(8,128)}, u32[]{:S(2)}) copy-start(f32[768,896]{1,0:T(8,128)} %fusion.17) | copy-start | bytes 8257540
  586.4 3.9 copy-start.1
Sparse Core Ops, SparseCore 0:
  9.7 104.5 all-gather.4
  116.7 67.4 all-gather.6
  210.3 55.4 reduce-scatter.9
  268.1 60.1 all-gather.10
  330.4 54.8 all-gather.8
  412.4 56.8 reduce-scatter.11
  473.6 112.7 reduce-scatter.13
